TPU v7x, 512 devices: a whole 4x8x8 slice. The times are simulated.
512 devices in a mesh: gx: 32 (over x_lo, y, core), row: 16 (over x_hi, z).
Axes of the slice: x: 4 (x_hi: 2, x_lo: 2; x = x_hi * 2 + x_lo), y: 8, z: 8, core: 2. Of those that a mesh axis runs over, the one named last changes fastest.
Arguments:
- test_vectors: float32 [2, 5, 64, 256, 128], P(None, None, 'gx', 'row')
- base_coeffs: float32 [101, 64, 256], P(None, 'gx', 'row'), as said below
- panel_set: float32 [512, 10, 10], P(('gx', 'row')), as said below
- owner_index: int32 [1], replicated, may hold values from 0 to 511
Outputs:
- basis: float32 [2, 5, 64, 128, 256], P(None, None, 'gx', 'row')
Inputs may be any that keep to these rules, and one draw needn't show every extreme that they name: `owner_index`: the index, with gx slowest, of the device whose panel this window uses. `panel_set`: panels are nonsingular. `base_coeffs`: viscosities are positive.
All inputs are finite; a program needn't handle non-finite values.
Results may differ from a plain program's by a relative error of at most 0.0003.
Values sent between devices are 32-bit elements; how exact they have to be, the bound alone decides.
No kernel may reach another device: no remote copies, remote signals or barrier semaphores. Data moves between devices by JAX's collectives and lax.ppermute only.
A program may use at most 64 MiB of HBM per device.

v0:
```python
import math
import jax
import jax.numpy as jnp
from jax import lax
from jax.sharding import PartitionSpec as P

STEPS = 2


def spread(value, axis, source):
    kept = jnp.where(lax.axis_index(axis) == source, value, 0).astype(value.dtype)
    return lax.psum(kept, axis)


def with_halo(block, sides, width):
    for axis, dim in sides:
        count = lax.axis_size(axis)
        forward = [(i, i + 1) for i in range(count - 1)]
        backward = [(target, source) for source, target in forward]
        low = lax.ppermute(
            lax.slice_in_dim(block, block.shape[dim] - width, None, axis=dim), axis, forward
        )
        high = lax.ppermute(lax.slice_in_dim(block, 0, width, axis=dim), axis, backward)
        block = jnp.concatenate([low, block, high], axis=dim)
    return block


def advance(padded, coeffs):
    n_var = padded.shape[1]
    n_pair = n_var * n_var
    advect = coeffs[: 3 * n_pair].reshape((3, n_var, n_var) + coeffs.shape[1:])
    reaction = coeffs[3 * n_pair : 4 * n_pair].reshape((n_var, n_var) + coeffs.shape[1:])
    viscous = coeffs[4 * n_pair]
    fluxes = jnp.einsum("djixr,kjxrt->dkixrt", advect, padded, precision=lax.Precision.HIGHEST)
    centre = padded[:, :, 1:-1, 1:-1]
    stream = fluxes[0, :, :, 2:, 1:-1] - fluxes[0, :, :, :-2, 1:-1]
    radial = fluxes[1, :, :, 1:-1, 2:] - fluxes[1, :, :, 1:-1, :-2]
    beside_all = fluxes[2, :, :, 1:-1, 1:-1]
    azimuth = jnp.roll(beside_all, -1, axis=4) - jnp.roll(beside_all, 1, axis=4)
    neighbours = (
        padded[:, :, 2:, 1:-1]
        + padded[:, :, :-2, 1:-1]
        + padded[:, :, 1:-1, 2:]
        + padded[:, :, 1:-1, :-2]
    )
    neighbours = neighbours + jnp.roll(centre, -1, axis=4) + jnp.roll(centre, 1, axis=4)
    source = jnp.einsum(
        "jixr,kjxrt->kixrt", reaction[:, :, 1:-1, 1:-1], centre, precision=lax.Precision.HIGHEST
    )
    return (
        centre
        + stream
        + radial
        + azimuth
        + viscous[1:-1, 1:-1, None] * (neighbours - 6.0 * centre)
        + source
    )


def body(test_vectors, base_coeffs, panel_set, owner_index):
    panel_now = spread(panel_set[0], ("gx", "row"), owner_index[0])
    field = test_vectors
    count_x = lax.axis_size("gx")
    count_r = lax.axis_size("row")
    wide_x = field.shape[2]
    wide_r = field.shape[3]
    n_theta = field.shape[4]
    n_var = field.shape[1]
    n_vec = field.shape[0]
    coeff_rim = with_halo(base_coeffs, (("gx", 1), ("row", 2)), 1)
    for repeat in range(STEPS):
        padded = with_halo(field, (("gx", 2), ("row", 3)), 1)
        field = advance(padded, coeff_rim)
    sketch = jnp.dot(panel_now, field.reshape(n_vec * n_var, -1), precision=lax.Precision.HIGHEST)
    first = sketch[:n_var]
    second = sketch[n_var:]
    norm_one = lax.psum(jnp.sum(first * first), ("gx", "row"))
    inv_one = 1.0 / jnp.sqrt(norm_one)
    unit_one = first * inv_one
    projection = lax.psum(jnp.sum(unit_one * second), ("gx", "row"))
    remainder = second - projection * unit_one
    norm_two = lax.psum(jnp.sum(remainder * remainder), ("gx", "row"))
    inv_two = 1.0 / jnp.sqrt(norm_two)
    scale = math.sqrt(n_var * wide_x * count_x * wide_r * count_r * n_theta)
    weight_one = scale * inv_one
    weight_two = scale * inv_two
    weight_mix = -scale * inv_two * projection * inv_one
    block_shape = (n_var, wide_x, wide_r, n_theta)
    column_one = first.reshape(block_shape)
    column_two = second.reshape(block_shape)
    basis_local = jnp.stack(
        [weight_one * column_one, weight_two * column_two + weight_mix * column_one]
    )
    return lax.all_to_all(
        basis_local.transpose(0, 1, 2, 4, 3), "row", split_axis=3, concat_axis=4, tiled=True
    )


def solution(mesh):
    placed = (
        P(None, None, "gx", "row", None),
        P(None, "gx", "row"),
        P(("gx", "row"), None, None),
        P(),
    )
    return jax.shard_map(
        body,
        mesh=mesh,
        in_specs=placed,
        out_specs=P(None, None, "gx", "row", None),
        check_vma=False,
    )
```

profile of v0, /device:TPU:2, one launch (start us, length us, event | category | flops | bytes accessed | tf_op | source)
XLA Modules:
  0.0 481.5 jit_solution(10872169300837984554)
XLA Ops:
  1.1 1.9 collective-permute-start
  3.1 5.8 %collective-permute-start.1 = (f32[2,5,1,16,128]{4,1,0,3,2:T(8,128)S(1)}, f32[2,5,1,16,128]{4,1,0,3,2:T(8,128)S(1)}, u32[]{:S(2)}, u32[]{:S(2)}) collective-permute-start(f32[2,5,1,16,128]{4,1,0,3,2:T(8,128)S(1)} %get-tuple-element.29), channel_id=1, source_target_pairs={{16,0},{32,16},{48,32},{64,48},{80,64},{96,80},{112,96},{128,112},... | collective-permute-start | bytes 245768 | tf_op jit(solution)/shard_map/ppermute | solution.py:23
  9.5 1.9 collective-permute-start.4
  11.4 5.8 %collective-permute-start.5 = (f32[101,1,16]{0,2,1:T(8,128)S(1)}, f32[101,1,16]{0,2,1:T(8,128)S(1)}, u32[]{:S(2)}, u32[]{:S(2)}) collective-permute-start(f32[101,1,16]{0,2,1:T(8,128)S(1)} %get-tuple-element.33), channel_id=1, source_target_pairs={{16,0},{32,16},{48,32},{64,48},{80,64},{96,80},{112,96},{128,112},... | collective-permute-start | bytes 19400 | tf_op jit(solution)/shard_map/ppermute | solution.py:23
  18.6 4.3 collective-permute-start.6
  22.8 1.3 collective-permute-start.7
  24.2 105.0 %psum.28 = f32[10,10]{1,0:T(8,128)S(1)} all-reduce(f32[10,10]{1,0:T(8,128)S(1)} %fusion.42), channel_id=1, replica_groups=mesh['gx'=32,'row'=16] {'gx','row'}, use_global_device_ids=true, to_apply=%region_0.1 | all-reduce | flops 100 | bytes 800 | tf_op jit(solution)/shard_map/psum | solution.py:12
  129.4 2.5 collective-permute-start.2
  131.9 1.3 collective-permute-start.3
  134.7 3.0 collective-permute-done.3
  137.7 1.5 convolution_bitcast_fusion.1
  140.2 1.9 collective-permute-start.8
  142.1 5.8 %collective-permute-start.9 = (f32[2,5,1,16,128]{4,1,0,3,2:T(8,128)S(1)}, f32[2,5,1,16,128]{4,1,0,3,2:T(8,128)S(1)}, u32[]{:S(2)}, u32[]{:S(2)}) collective-permute-start(f32[2,5,1,16,128]{4,1,0,3,2:T(8,128)S(1)} %get-tuple-element.20), channel_id=1, source_target_pairs={{16,0},{32,16},{48,32},{64,48},{80,64},{96,80},{112,96},{128,112},... | collective-permute-start | bytes 245768 | tf_op jit(solution)/shard_map/ppermute | solution.py:23
  148.6 1.8 collective-permute-done.9
  150.4 2.2 collective-permute-start.10
  154.2 4.2 collective-permute-done.11
  158.4 1.5 convolution_bitcast_fusion
  162.0 105.2 %psum.29 = f32[]{:T(128)} all-reduce(f32[]{:T(128)} %multiply_reduce_fusion.2), channel_id=1, replica_groups=mesh['gx'=32,'row'=16] {'gx','row'}, use_global_device_ids=true, to_apply=%region_2.3 | all-reduce | flops 1 | bytes 8 | tf_op jit(solution)/shard_map/psum | solution.py:77
  268.5 93.0 %psum.30 = f32[]{:T(128)} all-reduce(f32[]{:T(128)} %multiply_reduce_fusion.1), channel_id=1, replica_groups=mesh['gx'=32,'row'=16] {'gx','row'}, use_global_device_ids=true, to_apply=%region_4.5 | all-reduce | flops 1 | bytes 8 | tf_op jit(solution)/shard_map/psum | solution.py:80
  361.6 1.3 multiply_bitcast_fusion
  362.9 95.2 %psum.31 = f32[]{:T(128)} all-reduce(f32[]{:T(128)} %get-tuple-element.10), channel_id=1, replica_groups=mesh['gx'=32,'row'=16] {'gx','row'}, use_global_device_ids=true, to_apply=%region_6.7 | all-reduce | flops 1 | bytes 8 | tf_op jit(solution)/shard_map/psum | solution.py:82
  460.8 1.8 reshape.70
  462.6 14.1 %all_to_all.18 = f32[16,1,2560]{2,1,0:T(1,128)S(1)} all-to-all(f32[16,1,2560]{2,1,0:T(1,128)S(1)} %reshape.70), channel_id=1, replica_groups=mesh['gx'=32,'row'=16] {'row'}, dimensions={0} | all-to-all | bytes 327680 | tf_op jit(solution)/shard_map/all_to_all | solution.py:94
  478.3 1.7 reshape.71
  (67 shorter events, 14.4 us)
Async XLA Ops:
  0.0 129.2 %copy-start = (f32[2,5,2,16,128]{4,3,2,1,0:T(8,128)S(1)}, f32[2,5,2,16,128]{4,3,2,1,0:T(8,128)}, u32[]{:S(2)}) copy-start(f32[2,5,2,16,128]{4,3,2,1,0:T(8,128)} %param.4) | copy-start | bytes 491524
  0.0 18.2 %copy-start.1 = (f32[101,2,16]{0,2,1:T(8,128)S(1)}, f32[101,2,16]{0,2,1:T(8,128)}, u32[]{:S(2)}) copy-start(f32[101,2,16]{0,2,1:T(8,128)} %param.5) | copy-start | bytes 38788
  0.0 24.1 %copy-start.2 = (f32[1,10,10]{2,0,1:T(1,128)S(1)}, f32[1,10,10]{2,0,1:T(1,128)}, u32[]{:S(2)}) copy-start(f32[1,10,10]{2,0,1:T(1,128)} %param.6) | copy-start | bytes 1204
  1.1 128.1 %collective-permute-start = (f32[2,5,1,16,128]{4,1,0,3,2:T(8,128)S(1)}, f32[2,5,1,16,128]{4,1,0,3,2:T(8,128)S(1)}, u32[]{:S(2)}, u32[]{:S(2)}) collective-permute-start(f32[2,5,1,16,128]{4,1,0,3,2:T(8,128)S(1)} %get-tuple-element.30), channel_id=1, source_target_pairs={{0,16},{16,32},{32,48},{48,64},{64,80},{80,96},{96,112},{112,128},... | collective-permute-start | bytes 245768 | tf_op jit(solution)/shard_map/ppermute | solution.py:20
  3.1 126.3 %collective-permute-start.1 = (f32[2,5,1,16,128]{4,1,0,3,2:T(8,128)S(1)}, f32[2,5,1,16,128]{4,1,0,3,2:T(8,128)S(1)}, u32[]{:S(2)}, u32[]{:S(2)}) collective-permute-start(f32[2,5,1,16,128]{4,1,0,3,2:T(8,128)S(1)} %get-tuple-element.29), channel_id=1, source_target_pairs={{16,0},{32,16},{48,32},{64,48},{80,64},{96,80},{112,96},{128,112},... | collective-permute-start | bytes 245768 | tf_op jit(solution)/shard_map/ppermute | solution.py:23
  9.5 8.6 %collective-permute-start.4 = (f32[101,1,16]{0,2,1:T(8,128)S(1)}, f32[101,1,16]{0,2,1:T(8,128)S(1)}, u32[]{:S(2)}, u32[]{:S(2)}) collective-permute-start(f32[101,1,16]{0,2,1:T(8,128)S(1)} %get-tuple-element.34), channel_id=1, source_target_pairs={{0,16},{16,32},{32,48},{48,64},{64,80},{80,96},{96,112},{112,128},... | collective-permute-start | bytes 19400 | tf_op jit(solution)/shard_map/ppermute | solution.py:20
  11.4 7.1 %collective-permute-start.5 = (f32[101,1,16]{0,2,1:T(8,128)S(1)}, f32[101,1,16]{0,2,1:T(8,128)S(1)}, u32[]{:S(2)}, u32[]{:S(2)}) collective-permute-start(f32[101,1,16]{0,2,1:T(8,128)S(1)} %get-tuple-element.33), channel_id=1, source_target_pairs={{16,0},{32,16},{48,32},{64,48},{80,64},{96,80},{112,96},{128,112},... | collective-permute-start | bytes 19400 | tf_op jit(solution)/shard_map/ppermute | solution.py:23
  18.6 110.6 %collective-permute-start.6 = (f32[101,4,1]{0,2,1:T(1,128)S(1)}, f32[101,4,1]{0,2,1:T(1,128)S(1)}, u32[]{:S(2)}, u32[]{:S(2)}) collective-permute-start(f32[101,4,1]{0,2,1:T(1,128)S(1)} %get-tuple-element.31), channel_id=1, source_target_pairs={{0,1},{1,2},{2,3},{3,4},{4,5},{5,6},{6,7},{7,8},{8,9},{9,10},{10,1... | collective-permute-start | bytes 4856 | tf_op jit(solution)/shard_map/ppermute | solution.py:20
  22.8 106.4 %collective-permute-start.7 = (f32[101,4,1]{0,2,1:T(1,128)S(1)}, f32[101,4,1]{0,2,1:T(1,128)S(1)}, u32[]{:S(2)}, u32[]{:S(2)}) collective-permute-start(f32[101,4,1]{0,2,1:T(1,128)S(1)} %get-tuple-element.32), channel_id=1, source_target_pairs={{1,0},{2,1},{3,2},{4,3},{5,4},{6,5},{7,6},{8,7},{9,8},{10,9},{11,1... | collective-permute-start | bytes 4856 | tf_op jit(solution)/shard_map/ppermute | solution.py:23
  129.4 5.3 %collective-permute-start.2 = (f32[2,5,4,1,128]{4,1,0,3,2:T(8,128)S(1)}, f32[2,5,4,1,128]{4,1,0,3,2:T(8,128)S(1)}, u32[]{:S(2)}, u32[]{:S(2)}) collective-permute-start(f32[2,5,4,1,128]{4,1,0,3,2:T(8,128)S(1)} %get-tuple-element.8), channel_id=1, source_target_pairs={{0,1},{1,2},{2,3},{3,4},{4,5},{5,6},{6,7},{7,8},{8,9},{9,10},{10,1... | collective-permute-start | bytes 61448 | tf_op jit(solution)/shard_map/ppermute | solution.py:20
  131.9 5.8 %collective-permute-start.3 = (f32[2,5,4,1,128]{4,1,0,3,2:T(8,128)S(1)}, f32[2,5,4,1,128]{4,1,0,3,2:T(8,128)S(1)}, u32[]{:S(2)}, u32[]{:S(2)}) collective-permute-start(f32[2,5,4,1,128]{4,1,0,3,2:T(8,128)S(1)} %get-tuple-element.7), channel_id=1, source_target_pairs={{1,0},{2,1},{3,2},{4,3},{5,4},{6,5},{7,6},{8,7},{9,8},{10,9},{11,1... | collective-permute-start | bytes 61448 | tf_op jit(solution)/shard_map/ppermute | solution.py:23
  140.2 8.4 %collective-permute-start.8 = (f32[2,5,1,16,128]{4,1,0,3,2:T(8,128)S(1)}, f32[2,5,1,16,128]{4,1,0,3,2:T(8,128)S(1)}, u32[]{:S(2)}, u32[]{:S(2)}) collective-permute-start(f32[2,5,1,16,128]{4,1,0,3,2:T(8,128)S(1)} %get-tuple-element.19), channel_id=1, source_target_pairs={{0,16},{16,32},{32,48},{48,64},{64,80},{80,96},{96,112},{112,128},... | collective-permute-start | bytes 245768 | tf_op jit(solution)/shard_map/ppermute | solution.py:20
  142.1 8.3 %collective-permute-start.9 = (f32[2,5,1,16,128]{4,1,0,3,2:T(8,128)S(1)}, f32[2,5,1,16,128]{4,1,0,3,2:T(8,128)S(1)}, u32[]{:S(2)}, u32[]{:S(2)}) collective-permute-start(f32[2,5,1,16,128]{4,1,0,3,2:T(8,128)S(1)} %get-tuple-element.20), channel_id=1, source_target_pairs={{16,0},{32,16},{48,32},{64,48},{80,64},{96,80},{112,96},{128,112},... | collective-permute-start | bytes 245768 | tf_op jit(solution)/shard_map/ppermute | solution.py:23
  150.4 3.8 collective-permute-start.10
  152.6 5.8 %collective-permute-start.11 = (f32[2,5,4,1,128]{4,1,0,3,2:T(8,128)S(1)}, f32[2,5,4,1,128]{4,1,0,3,2:T(8,128)S(1)}, u32[]{:S(2)}, u32[]{:S(2)}) collective-permute-start(f32[2,5,4,1,128]{4,1,0,3,2:T(8,128)S(1)} %get-tuple-element.5), channel_id=1, source_target_pairs={{1,0},{2,1},{3,2},{4,3},{5,4},{6,5},{7,6},{8,7},{9,8},{10,9},{11,1... | collective-permute-start | bytes 61448 | tf_op jit(solution)/shard_map/ppermute | solution.py:23
where the time goes:
time: 483 us; the launch traced here: 482 us
  blocking collectives  413 us (86%)
  starting transfers between devices  35.8 us (7%)
  local copies, waits for them, and re-layouts  11.6 us (2%)
  waiting for transfers between devices  10.1 us (2%)
    psum x1, blocking collectives, body(): norm_one = lax.psum(jnp.sum(first * first), ('gx', 'row'))  105 us
    psum x1, blocking collectives, spread(): return lax.psum(kept, axis)  105 us
    psum x1, blocking collectives, body(): norm_two = lax.psum(jnp.sum(remainder * remainder), ('gx', 'row'))  95.2 us
    psum x1, blocking collectives, body(): projection = lax.psum(jnp.sum(unit_one * second), ('gx', 'row'))  93 us
    ppermute x6, starting transfers between devices, with_halo(): lax.ppermute(lax.slice_in_dim(block, 0, width, axis=dim), axis, backward)  21.1 us
    ppermute x6, starting transfers between devices, with_halo(): lax.ppermute(lax.slice_in_dim(block, block.shape[dim] - width, None, axis...  14.7 us
    all_to_all x1, blocking collectives, body(): lax.all_to_all(basis_local.transpose(0, 1, 2, 4, 3), 'row', split_axis=3,...  14.1 us
  transfers between devices with their start and end apart: 12, of which 6 were waited for; matrix products, arithmetic and copies ran while one was open for 1% of the time, Pallas kernels for 0%

commit v1 on v0

--- a/solution.py
+++ b/solution.py
@@ -9,7 +9,7 @@
 
 def spread(value, axis, source):
     kept = jnp.where(lax.axis_index(axis) == source, value, 0).astype(value.dtype)
-    return lax.psum(kept, axis)
+    return jnp.sum(lax.all_gather(kept, axis), axis=0)
 
 
 def with_halo(block, sides, width):

time: 483 us -> 1760 us (3.64)
  blocking collectives: 413 us -> 1680 us
    all_gather x0 -> x1, blocking collectives: none -> 1220 us  [spread(): return jnp.sum(lax.all_gather(kept, axis), axis=0)]
    psum x1, blocking collectives: 105 us -> 258 us  [body(): norm_one = lax.psum(jnp.sum(first * first), ('gx', 'row'))]
    psum x1 -> x0, blocking collectives: 105 us -> none  [spread(): return lax.psum(kept, axis)]
  transfers between devices with their start and end apart: 12 -> 12, of which waited for: 6 -> 6; matrix products, arithmetic and copies ran while one was open for 1% -> 0% of each run, Pallas kernels for 0% -> 0%
where the time goes in v1:
time: 1760 us
  blocking collectives  1680 us (95%)
  starting transfers between devices  34.6 us (2%)
  waiting for transfers between devices  18.6 us (1%)
    all_gather x1, blocking collectives, spread(): return jnp.sum(lax.all_gather(kept, axis), axis=0)  1220 us
    psum x1, blocking collectives, body(): norm_one = lax.psum(jnp.sum(first * first), ('gx', 'row'))  258 us
    psum x1, blocking collectives, body(): norm_two = lax.psum(jnp.sum(remainder * remainder), ('gx', 'row'))  96.2 us
    psum x1, blocking collectives, body(): projection = lax.psum(jnp.sum(unit_one * second), ('gx', 'row'))  95.3 us
  transfers between devices with their start and end apart: 12, of which 6 were waited for; matrix products, arithmetic and copies ran while one was open for 0% of the time, Pallas kernels for 0%

profile of v1, /device:TPU:2, one launch (start us, length us, event | category | flops | bytes accessed | tf_op | source)
XLA Modules:
  0.0 1761.0 jit_solution(15314460530052584973)
XLA Ops:
  1.1 1.9 collective-permute-start
  3.0 5.8 collective-permute-start.1
  9.5 1.9 collective-permute-start.4
  11.4 5.8 collective-permute-start.5
  18.5 4.3 collective-permute-start.6
  22.8 1.3 collective-permute-start.7
  24.1 1217.8 %all_gather.4 = f32[512,10,10]{2,1,0:T(8,128)} all-gather(f32[1,10,10]{2,1,0:T(8,128)S(1)} %copy_select_fusion), channel_id=1, replica_groups=mesh['gx'=32,'row'=16] {'gx','row'}, dimensions={0}, use_global_device_ids=true | all-gather | bytes 205200 | tf_op jit(solution)/shard_map/all_gather | solution.py:12
  1241.9 2.8 reduce_sum.36
  1245.0 1.8 collective-permute-start.2
  1249.6 4.2 collective-permute-done.3
  1253.8 1.5 convolution_bitcast_fusion.1
  1256.3 1.9 collective-permute-start.8
  1258.2 5.8 collective-permute-start.9
  1264.7 9.0 collective-permute-done.9
  1273.7 1.6 collective-permute-start.10
  1276.9 4.2 collective-permute-done.11
  1281.2 1.5 convolution_bitcast_fusion
  1284.8 258.2 %psum.21 = f32[]{:T(128)} all-reduce(f32[]{:T(128)} %multiply_reduce_fusion.2), channel_id=1, replica_groups=mesh['gx'=32,'row'=16] {'gx','row'}, use_global_device_ids=true, to_apply=%region_2.3 | all-reduce | flops 1 | bytes 8 | tf_op jit(solution)/shard_map/psum | solution.py:77
  1544.3 95.3 %psum.22 = f32[]{:T(128)} all-reduce(f32[]{:T(128)} %multiply_reduce_fusion.1), channel_id=1, replica_groups=mesh['gx'=32,'row'=16] {'gx','row'}, use_global_device_ids=true, to_apply=%region_4.5 | all-reduce | flops 1 | bytes 8 | tf_op jit(solution)/shard_map/psum | solution.py:80
  1639.5 1.3 multiply_bitcast_fusion
  1640.9 96.2 %psum.23 = f32[]{:T(128)} all-reduce(f32[]{:T(128)} %get-tuple-element.10), channel_id=1, replica_groups=mesh['gx'=32,'row'=16] {'gx','row'}, use_global_device_ids=true, to_apply=%region_6.7 | all-reduce | flops 1 | bytes 8 | tf_op jit(solution)/shard_map/psum | solution.py:82
  1739.8 1.8 reshape.67
  1741.6 14.5 all_to_all.18
  1757.7 1.7 reshape.68
  (68 shorter events, 15.6 us)
Async XLA Ops:
  0.0 18.1 %copy-start.1 = (f32[101,2,16]{0,2,1:T(8,128)S(1)}, f32[101,2,16]{0,2,1:T(8,128)}, u32[]{:S(2)}) copy-start(f32[101,2,16]{0,2,1:T(8,128)} %param.5) | copy-start | bytes 38788
  0.0 18.1 %copy-start.2 = (f32[1,10,10]{2,0,1:T(1,128)S(1)}, f32[1,10,10]{2,0,1:T(1,128)}, u32[]{:S(2)}) copy-start(f32[1,10,10]{2,0,1:T(1,128)} %param.6) | copy-start | bytes 1204
  1.1 1243.7 %collective-permute-start = (f32[2,5,1,16,128]{4,1,0,3,2:T(8,128)S(1)}, f32[2,5,1,16,128]{4,1,0,3,2:T(8,128)S(1)}, u32[]{:S(2)}, u32[]{:S(2)}) collective-permute-start(f32[2,5,1,16,128]{4,1,0,3,2:T(8,128)S(1)} %get-tuple-element.30), channel_id=1, source_target_pairs={{0,16},{16,32},{32,48},{48,64},{64,80},{80,96},{96,112},{112,128},... | collective-permute-start | bytes 245768 | tf_op jit(solution)/shard_map/ppermute | solution.py:20
  3.0 1241.9 %collective-permute-start.1 = (f32[2,5,1,16,128]{4,1,0,3,2:T(8,128)S(1)}, f32[2,5,1,16,128]{4,1,0,3,2:T(8,128)S(1)}, u32[]{:S(2)}, u32[]{:S(2)}) collective-permute-start(f32[2,5,1,16,128]{4,1,0,3,2:T(8,128)S(1)} %get-tuple-element.29), channel_id=1, source_target_pairs={{16,0},{32,16},{48,32},{64,48},{80,64},{96,80},{112,96},{128,112},... | collective-permute-start | bytes 245768 | tf_op jit(solution)/shard_map/ppermute | solution.py:23
  9.5 8.6 collective-permute-start.4
  11.4 7.1 collective-permute-start.5
  18.5 1226.2 %collective-permute-start.6 = (f32[101,4,1]{0,2,1:T(1,128)S(1)}, f32[101,4,1]{0,2,1:T(1,128)S(1)}, u32[]{:S(2)}, u32[]{:S(2)}) collective-permute-start(f32[101,4,1]{0,2,1:T(1,128)S(1)} %get-tuple-element.31), channel_id=1, source_target_pairs={{0,1},{1,2},{2,3},{3,4},{4,5},{5,6},{6,7},{7,8},{8,9},{9,10},{10,1... | collective-permute-start | bytes 4856 | tf_op jit(solution)/shard_map/ppermute | solution.py:20
  22.8 1221.9 %collective-permute-start.7 = (f32[101,4,1]{0,2,1:T(1,128)S(1)}, f32[101,4,1]{0,2,1:T(1,128)S(1)}, u32[]{:S(2)}, u32[]{:S(2)}) collective-permute-start(f32[101,4,1]{0,2,1:T(1,128)S(1)} %get-tuple-element.32), channel_id=1, source_target_pairs={{1,0},{2,1},{3,2},{4,3},{5,4},{6,5},{7,6},{8,7},{9,8},{10,9},{11,1... | collective-permute-start | bytes 4856 | tf_op jit(solution)/shard_map/ppermute | solution.py:23
  1241.9 2.9 copy-start
  1245.0 4.7 collective-permute-start.2
  1246.8 7.0 collective-permute-start.3
  1256.3 8.4 collective-permute-start.8
  1258.2 15.5 collective-permute-start.9
  1273.7 3.2 collective-permute-start.10
  1275.4 5.8 collective-permute-start.11
